TPU v7x, 32 devices: a whole 2x2x4 slice. The times are simulated.
32 devices in a mesh: row: 8 (over y, x, core), col: 4 (over z).
Axes of the slice: x: 2, y: 2, z: 4, core: 2. Of those that a mesh axis runs over, the one named last changes fastest.
Arguments:
- tiles: bfloat16 [8, 4, 80, 256, 256], P('row', 'col'), may hold values from -0.125 to 0.125
- tile_coords: int32 [2, 8, 4, 80], P(None, 'row', 'col'), may hold values from 0 to 1023, as said below
- tile_counts: int32 [8, 4], P('row', 'col'), may hold values from 40 to 80, as said below
- vectors: bfloat16 [262144, 16], P(('row', 'col')), may hold values from -6 to 6
Outputs:
- product: float32 [262144, 16], P(('row', 'col'))
Inputs may be any that keep to these rules, and one draw needn't show every extreme that they name: `tile_coords`: for slot s below tile_counts[r, c]: the tile row I lies in r * 128 to (r + 1) * 128 - 1; the tile column J has (J // 32) % 4 equal to c; when I != J, I < J exactly when I + J is even; no (row, column) pair appears in two live slots anywhere. Among the live slots of one device at most 35 have tile rows in any one run of 32 tile rows, and at most 28 have tile columns in any one run of 32 tile columns; a device with all slots live reaches both. Slots at or above the count hold 0. `tile_counts`: some device holds exactly 80 live slots.
All inputs are finite; a program needn't handle non-finite values.
Results may differ from a plain program's by a relative error of at most 0.0075.
Values may be sent and summed in bfloat16 or wider, within the bound.
A program may use at most 320 MiB of HBM per device.

v0:
```python
import jax
import jax.numpy as jnp
from jax import lax
from jax.sharding import PartitionSpec as P


def split_tile(stored, tile_rows, tile_cols):
    size_tile = stored.shape[-1]
    down_idx = jnp.arange(size_tile, dtype=jnp.int32)[:, None]
    across_idx = jnp.arange(size_tile, dtype=jnp.int32)[None, :]
    off_diag = (tile_rows != tile_cols)[:, None, None]
    zero_val = jnp.zeros((), stored.dtype)
    upper_part = jnp.where(off_diag | (down_idx <= across_idx)[None], stored, zero_val)
    lower_part = jnp.where(off_diag | (down_idx < across_idx)[None], stored, zero_val)
    return (upper_part, lower_part)


def shards(tiles, tile_coords, tile_counts, vectors):
    size_tile = tiles.shape[-1]
    slot_count = tiles.shape[2]
    vector_width = vectors.shape[1]
    per_slab = vectors.shape[0] // size_tile
    cols_count = lax.axis_size("col")
    row_here = lax.axis_index("row")
    col_here = lax.axis_index("col")
    stored = tiles.reshape(slot_count, size_tile, size_tile)
    tile_rows = tile_coords[0].reshape(slot_count)
    tile_cols = tile_coords[1].reshape(slot_count)
    live_slots = jnp.arange(slot_count, dtype=jnp.int32) < tile_counts.reshape(())
    row_block = lax.all_gather(vectors, "col", axis=0, tiled=True).reshape(
        -1, size_tile, vector_width
    )
    col_group = lax.all_gather(vectors, "row", axis=0, tiled=True).reshape(
        -1, size_tile, vector_width
    )
    row_local = jnp.where(live_slots, tile_rows - row_here * cols_count * per_slab, 0)
    col_local = tile_cols // per_slab // cols_count * per_slab + tile_cols % per_slab
    col_local = jnp.where(live_slots, col_local, 0)
    upper_part, lower_part = split_tile(stored, tile_rows, tile_cols)
    apply_operator = jnp.einsum(
        "tab,tbv->tav", upper_part, col_group[col_local], preferred_element_type=jnp.float32
    ).astype(jnp.bfloat16)
    mirror = jnp.einsum(
        "tba,tbv->tav", lower_part, row_block[row_local], preferred_element_type=jnp.float32
    ).astype(jnp.bfloat16)
    zero_val = jnp.zeros((), jnp.bfloat16)
    apply_operator = jnp.where(live_slots[:, None, None], apply_operator, zero_val).reshape(
        slot_count, size_tile * vector_width
    )
    mirror = jnp.where(live_slots[:, None, None], mirror, zero_val).reshape(
        slot_count, size_tile * vector_width
    )
    local_row_range = per_slab * size_tile
    panel_start = (row_here * cols_count + col_here) * per_slab
    row_targets = jnp.where(live_slots, tile_rows, -1)
    col_targets = jnp.where(live_slots, tile_cols, -1)

    def merge_into_panel(pieces_in):
        products, destination_rows = pieces_in
        wanted = panel_start + jnp.arange(per_slab, dtype=jnp.int32)
        onehot = (destination_rows[:, None] == wanted[None, :]).astype(jnp.bfloat16)
        return jnp.einsum("ts,tk->sk", onehot, products, preferred_element_type=jnp.float32)

    owned_direct = merge_into_panel(
        (
            lax.all_gather(apply_operator, "col", axis=0, tiled=True),
            lax.all_gather(row_targets, "col", axis=0, tiled=True),
        )
    )
    owned_reflected = merge_into_panel(
        (
            lax.all_gather(mirror, "row", axis=0, tiled=True),
            lax.all_gather(col_targets, "row", axis=0, tiled=True),
        )
    )
    owned_direct = owned_direct.reshape(local_row_range, vector_width)
    owned_reflected = owned_reflected.reshape(local_row_range, vector_width)
    return owned_direct + owned_reflected


def solution(mesh):
    in_specs = (
        P("row", "col", None, None, None),
        P(None, "row", "col", None),
        P("row", "col"),
        P(("row", "col"), None),
    )
    out_specs = P(("row", "col"), None)
    return jax.shard_map(shards, mesh=mesh, in_specs=in_specs, out_specs=out_specs, check_vma=False)
```

profile of v0, /device:TPU:0, one launch (start us, length us, event | category | flops | bytes accessed | tf_op | source)
XLA Modules:
  0.0 183.4 jit_solution(3489110521087887098)
XLA Ops:
  6.5 0.0 all-gather.5.cloned.1.call-start
  6.5 0.7 all-gather.5.cloned.1.call-update
  7.3 0.0 all-gather.9.cloned.1.call-start
  7.3 0.7 all-gather.9.cloned.1.call-update
  8.0 0.0 all-gather.7.cloned.1.call-start
  8.7 0.7 fusion.23
  9.4 0.7 bitcast_compare_fusion
  10.1 29.8 %all-gather.5.cloned.1.call-done = bf16[65536,16]{0,1:T(8,128)(2,1)} async-done(((bf16[8192,16]{0,1:T(8,128)(2,1)}), bf16[65536,16]{0,1:T(8,128)(2,1)}) %all-gather.5.cloned.1.call-update) | async-done | bytes 2097168 | tf_op jit(solution)/shard_map/all_gather | solution.py:33
  39.9 1.7 copy.25
  41.6 0.6 gather_fusion
  42.3 6.9 %fusion.12 = bf16[80,256,16]{1,2,0:T(8,128)(2,1)S(1)} fusion(bf16[80,256,16]{1,2,0:T(8,128)(2,1)S(1)} %gather_fusion, bf16[1,1,80,256,256]{4,3,2,1,0:T(8,128)(2,1)} %param.4, pred[256,256]{1,0:T(8,128)(4,1)S(1)} %iota_compare_fusion.1, pred[80]{0:T(512)(128)(4,1)S(1)} %get-tuple-element.9, pred[80]{0:T(512)(128)(4,1)S(1)} %get-tuple-element.10), kind=kOutput, calls=%fused_computation.18 | convolution fusion | flops 178913280 | bytes 11862176 | tf_op jit(solution)/shard_map/tab,tbv->tav/dot_general | solution.py:40
  49.2 1.3 copy.15
  50.5 1.3 copy.16
  51.8 0.0 all-gather.7.cloned.1.call-update
  51.8 0.0 all-gather.11.cloned.1.call-start
  51.9 17.5 %all-gather.9.cloned.1.call-done = bf16[32768,16]{0,1:T(8,128)(2,1)} async-done(((bf16[8192,16]{0,1:T(8,128)(2,1)}), bf16[32768,16]{0,1:T(8,128)(2,1)}) %all-gather.9.cloned.1.call-update) | async-done | bytes 1048592 | tf_op jit(solution)/shard_map/all_gather | solution.py:30
  69.4 1.3 copy.26
  70.7 0.6 gather_fusion.1
  71.3 0.0 copy-start.2
  71.4 0.0 copy-start.1
  71.4 0.0 copy-start
  71.4 5.6 %fusion.13 = bf16[80,256,16]{1,2,0:T(8,128)(2,1)S(1)} fusion(bf16[80,256,16]{1,2,0:T(8,128)(2,1)S(1)} %gather_fusion.1, bf16[1,1,80,256,256]{4,3,2,1,0:T(8,128)(2,1)} %param.4, pred[256,256]{1,0:T(8,128)(4,1)S(1)} %iota_compare_fusion, pred[80]{0:T(512)(128)(4,1)S(1)} %get-tuple-element.9, pred[80]{0:T(512)(128)(4,1)S(1)} %get-tuple-element.10), kind=kOutput, calls=%fused_computation.19 | convolution fusion | flops 178913280 | bytes 11862176 | tf_op jit(solution)/shard_map/tba,tbv->tav/dot_general | solution.py:43
  77.0 1.3 copy.18
  78.3 1.2 copy.19
  79.5 0.0 all-gather.11.cloned.1.call-update
  79.6 0.0 copy-done.2
  79.6 0.7 dynamic-slice
  80.2 0.0 copy-done.1
  80.2 0.6 dynamic-slice.1
  82.3 0.0 copy-done
  82.3 0.1 fusion.24
  82.4 7.9 %all-reduce = s32[320]{0:T(512)S(1)} all-reduce(s32[320]{0:T(512)S(1)} %get-tuple-element.6), channel_id=1, replica_groups=mesh['row'=8,'col'=4] {'col'}, use_global_device_ids=true, to_apply=%add | all-reduce | flops 320 | bytes 2560
  90.3 8.0 %all-reduce.1 = s32[640]{0:T(1024)S(1)} all-reduce(s32[640]{0:T(1024)S(1)} %get-tuple-element.5), channel_id=1, replica_groups=mesh['row'=8,'col'=4] {'row'}, use_global_device_ids=true, to_apply=%add.1 | all-reduce | flops 640 | bytes 5120
  98.3 27.2 %all-gather.7.cloned.1.call-done = bf16[320,4096]{1,0:T(8,128)(2,1)} async-done(((bf16[80,4096]{1,0:T(8,128)(2,1)}), bf16[320,4096]{1,0:T(8,128)(2,1)}) %all-gather.7.cloned.1.call-update) | async-done | bytes 2621456 | tf_op jit(solution)/shard_map/all_gather | solution.py:66
  125.5 2.4 %fusion.17 = f32[32,4096]{1,0:T(8,128)S(1)} fusion(bf16[320,4096]{1,0:T(8,128)(2,1)} %all-gather.7.cloned.1.call-done, s32[32]{0:T(128)S(1)} %iota_add_fusion, s32[320]{0:T(512)S(1)} %all-reduce), kind=kOutput, calls=%fused_computation.26 | convolution fusion | flops 83896320 | bytes 3147136 | tf_op jit(solution)/shard_map/ts,tk->sk/dot_general | solution.py:62
  127.9 39.2 %all-gather.11.cloned.1.call-done = bf16[640,4096]{1,0:T(8,128)(2,1)} async-done(((bf16[80,4096]{1,0:T(8,128)(2,1)}), bf16[640,4096]{1,0:T(8,128)(2,1)}) %all-gather.11.cloned.1.call-update) | async-done | bytes 5242896 | tf_op jit(solution)/shard_map/all_gather | solution.py:72
  167.1 3.5 %convolution_add_fusion = f32[32,4096]{1,0:T(8,128)S(1)} fusion(f32[32,4096]{1,0:T(8,128)S(1)} %fusion.17, bf16[640,4096]{1,0:T(8,128)(2,1)} %all-gather.11.cloned.1.call-done, s32[32]{0:T(128)S(1)} %iota_add_fusion, s32[640]{0:T(1024)S(1)} %all-reduce.1), kind=kOutput, calls=%fused_computation.14 | convolution fusion | flops 167923712 | bytes 6294144 | tf_op jit(solution)/shard_map/ts,tk->sk/dot_general | solution.py:62
  170.6 2.8 %add.96 = f32[8192,16]{1,0:T(8,128)} reshape(f32[32,4096]{1,0:T(8,128)S(1)} %convolution_add_fusion) | data formatting | bytes 1048576 | tf_op jit(solution)/shard_map/add | solution.py:78
  173.4 3.5 %copy.20 = f32[8192,16]{0,1:T(8,128)} copy(f32[8192,16]{1,0:T(8,128)} %add.96) | data formatting | bytes 1048576 | tf_op jit(solution)/shard_map/add | solution.py:78
  (7 shorter events, 0.1 us)
Async XLA Ops:
  6.5 33.4 %all-gather.5.cloned.1.call-start = ((), (), s32[]{:S(2)}) async-start(), calls=%async_computation | async-start | bytes 2359296 | tf_op jit(solution)/shard_map/all_gather | solution.py:33
  7.3 62.2 %all-gather.9.cloned.1.call-start = ((), (), s32[]{:S(2)}) async-start(), calls=%async_computation.2 | async-start | bytes 1310720 | tf_op jit(solution)/shard_map/all_gather | solution.py:30
  8.0 117.5 %all-gather.7.cloned.1.call-start = ((), (), s32[]{:S(2)}) async-start(), calls=%async_computation.1 | async-start | bytes 3276800 | tf_op jit(solution)/shard_map/all_gather | solution.py:66
  51.8 115.3 %all-gather.11.cloned.1.call-start = ((), (), s32[]{:S(2)}) async-start(), calls=%async_computation.3 | async-start | bytes 5898240 | tf_op jit(solution)/shard_map/all_gather | solution.py:72
  71.3 8.2 %copy-start.2 = (u32[32]{0:T(128)S(1)}, u32[32]{0:T(128)}, u32[]{:S(2)}) copy-start(u32[32]{0:T(128)} %constant.65) | copy-start | bytes 388
  71.4 8.9 %copy-start.1 = (u32[32]{0:T(128)S(1)}, u32[32]{0:T(128)}, u32[]{:S(2)}) copy-start(u32[32]{0:T(128)} %constant.70) | copy-start | bytes 388
  71.4 10.9 %copy-start = (s32[2,1,1,80]{3,2,1,0:T(1,128)S(1)}, s32[2,1,1,80]{3,2,1,0:T(1,128)}, u32[]{:S(2)}) copy-start(s32[2,1,1,80]{3,2,1,0:T(1,128)} %param.5) | copy-start | bytes 1924
Sparse Core Ops, SparseCore 0:
  9.3 30.5 all-gather.4
  41.5 27.9 all-gather.8
  71.0 54.4 all-gather.6
  127.2 39.8 all-gather.10
where the time goes:
time: 184 us; the launch traced here: 183 us
  waiting for transfers between devices  115 us (62%)
  matrix products  18.5 us (10%)
  local copies, waits for them, and re-layouts  17 us (9%)
  blocking collectives  15.9 us (9%)
  between operations  15.3 us (8%)
    all_gather x1, waiting for transfers between devices, shards(): lax.all_gather(mirror, 'row', axis=0, tiled=True)  39.2 us
    all_gather x1, waiting for transfers between devices, shards(): lax.all_gather(vectors, 'row', axis=0, tiled=True)  29.8 us
    all_gather x1, waiting for transfers between devices, shards(): lax.all_gather(apply_operator, 'col', axis=0, tiled=True)  27.2 us
    all_gather x1, waiting for transfers between devices, shards(): lax.all_gather(vectors, 'col', axis=0, tiled=True)  17.5 us
    unnamed x2, blocking collectives  15.9 us
    dot_general x1, matrix products, shards(): jnp.einsum('tab,tbv->tav', upper_part, col_group[col_local], preferred_el...  6.91 us
    add x2, local copies, waits for them, and re-layouts, shards(): return owned_direct + owned_reflected  6.27 us
    dot_general x2, matrix products, merge_into_panel(): jnp.einsum('ts,tk->sk', onehot, products, preferred_element_type=jnp.floa...  5.94 us
  transfers between devices with their start and end apart: 4, of which 4 were waited for; matrix products, arithmetic and copies ran while one was open for 15% of the time, Pallas kernels for 0%

commit v1 on v0

--- a/solution.py
+++ b/solution.py
@@ -2,6 +2,27 @@
 import jax.numpy as jnp
 from jax import lax
 from jax.sharding import PartitionSpec as P
+
+
+def collect(x, axis, dim):
+    length, index, extent = (lax.axis_size(axis), lax.axis_index(axis), x.shape[dim])
+    upward = [(i, (i + 1) % length) for i in range(length)]
+    left = [(i, (i - 1) % length) for i in range(length)]
+    result = jnp.zeros((*x.shape[:dim], length * extent, *x.shape[dim + 1 :]), x.dtype)
+    result = lax.dynamic_update_slice_in_dim(result, x, index * extent, axis=dim)
+    from_left = from_right = x
+    middle = length // 2
+    for hop in range(1, middle + 1):
+        from_left = lax.ppermute(from_left, axis, upward)
+        result = lax.dynamic_update_slice_in_dim(
+            result, from_left, (index - hop) % length * extent, axis=dim
+        )
+        if hop < length - middle:
+            from_right = lax.ppermute(from_right, axis, left)
+            result = lax.dynamic_update_slice_in_dim(
+                result, from_right, (index + hop) % length * extent, axis=dim
+            )
+    return result
 
 
 def split_tile(stored, tile_rows, tile_cols):
@@ -27,9 +48,7 @@
     tile_rows = tile_coords[0].reshape(slot_count)
     tile_cols = tile_coords[1].reshape(slot_count)
     live_slots = jnp.arange(slot_count, dtype=jnp.int32) < tile_counts.reshape(())
-    row_block = lax.all_gather(vectors, "col", axis=0, tiled=True).reshape(
-        -1, size_tile, vector_width
-    )
+    row_block = collect(vectors, "col", 0).reshape(-1, size_tile, vector_width)
     col_group = lax.all_gather(vectors, "row", axis=0, tiled=True).reshape(
         -1, size_tile, vector_width
     )

time: 184 us -> 165 us (0.90)
  waiting for transfers between devices: 115 us -> 93.1 us
  starting transfers between devices: 0.12 us -> 6.72 us
  blocking collectives: 15.9 us -> 13.9 us
    all_gather x1 -> x0, waiting for transfers between devices: 17.5 us -> none  [shards(): lax.all_gather(vectors, 'col', axis=0, tiled=True)]
    ppermute x0 -> x3, waiting for transfers between devices: none -> 8.72 us  [the longest x2 8.72 us: collect(): from_left = lax.ppermute(from_left, axis, upward)]
    all_gather x1, waiting for transfers between devices: 27.2 us -> 18.8 us  [shards(): lax.all_gather(apply_operator, 'col', axis=0, tiled=True)]
    ppermute x0 -> x3, starting transfers between devices: none -> 6.64 us  [the longest x1 5.1 us: collect(): from_right = lax.ppermute(from_right, axis, left)]
    all_gather x1, waiting for transfers between devices: 29.8 us -> 25.4 us  [shards(): lax.all_gather(vectors, 'row', axis=0, tiled=True)]
    unnamed x2, blocking collectives: 15.9 us -> 13.9 us
  transfers between devices with their start and end apart: 4 -> 6, of which waited for: 4 -> 4; matrix products, arithmetic and copies ran while one was open for 15% -> 16% of each run, Pallas kernels for 0% -> 0%
where the time goes in v1:
time: 165 us
  waiting for transfers between devices  93.1 us (56%)
  matrix products  18.5 us (11%)
  local copies, waits for them, and re-layouts  15.9 us (10%)
  between operations  15.3 us (9%)
  blocking collectives  13.9 us (8%)
  starting transfers between devices  6.72 us (4%)
    all_gather x1, waiting for transfers between devices, shards(): lax.all_gather(mirror, 'row', axis=0, tiled=True)  39.3 us
    all_gather x1, waiting for transfers between devices, shards(): lax.all_gather(vectors, 'row', axis=0, tiled=True)  25.4 us
    all_gather x1, waiting for transfers between devices, shards(): lax.all_gather(apply_operator, 'col', axis=0, tiled=True)  18.8 us
    unnamed x2, blocking collectives  13.9 us
    ppermute x2, waiting for transfers between devices, collect(): from_left = lax.ppermute(from_left, axis, upward)  8.72 us
    dot_general x1, matrix products, shards(): jnp.einsum('tab,tbv->tav', upper_part, col_group[col_local], preferred_el...  6.91 us
    add x2, local copies, waits for them, and re-layouts, shards(): return owned_direct + owned_reflected  6.27 us
    dot_general x2, matrix products, merge_into_panel(): jnp.einsum('ts,tk->sk', onehot, products, preferred_element_type=jnp.floa...  5.94 us
  transfers between devices with their start and end apart: 6, of which 4 were waited for; matrix products, arithmetic and copies ran while one was open for 16% of the time, Pallas kernels for 0%

profile of v1, /device:TPU:0, one launch (start us, length us, event | category | flops | bytes accessed | tf_op | source)
XLA Modules:
  0.0 165.0 jit_solution(10316947326568994016)
XLA Ops:
  6.5 0.0 all-gather.4.cloned.1.call-start
  6.5 0.7 all-gather.4.cloned.1.call-update
  7.3 0.0 all-gather.6.cloned.1.call-start
  7.3 5.1 %collective-permute-start.1 = (bf16[8192,16]{0,1:T(8,128)(2,1)}, bf16[8192,16]{0,1:T(8,128)(2,1)S(1)}, u32[]{:S(2)}, u32[]{:S(2)}) collective-permute-start(bf16[8192,16]{0,1:T(8,128)(2,1)} %param.7), channel_id=1, source_target_pairs={{0,3},{1,0},{2,1},{3,2},{4,7},{5,4},{6,5},{7,6},{8,11},{9,8},{10,9... | collective-permute-start | bytes 786440 | tf_op jit(solution)/shard_map/ppermute | solution.py:21
  12.4 0.0 collective-permute-start
  13.1 0.7 fusion.23
  13.8 0.7 bitcast_compare_fusion
  14.5 25.4 %all-gather.4.cloned.1.call-done = bf16[65536,16]{0,1:T(8,128)(2,1)} async-done(((bf16[8192,16]{0,1:T(8,128)(2,1)}), bf16[65536,16]{0,1:T(8,128)(2,1)}) %all-gather.4.cloned.1.call-update) | async-done | bytes 2097168 | tf_op jit(solution)/shard_map/all_gather | solution.py:52
  39.9 1.7 %copy.25 = bf16[2,256,8,256]{3,2,0,1:T(8,128)(2,1)S(1)} copy(bf16[2,256,8,256]{3,2,1,0:T(8,128)(2,1)} %bitcast.73) | data formatting | bytes 4194304 | tf_op jit(solution)/shard_map/reshape | solution.py:52
  41.6 0.6 gather_fusion
  42.3 6.9 %fusion.12 = bf16[80,256,16]{1,2,0:T(8,128)(2,1)S(1)} fusion(bf16[80,256,16]{1,2,0:T(8,128)(2,1)S(1)} %gather_fusion, bf16[1,1,80,256,256]{4,3,2,1,0:T(8,128)(2,1)} %param.4, pred[256,256]{1,0:T(8,128)(4,1)S(1)} %iota_compare_fusion.1, pred[80]{0:T(512)(128)(4,1)S(1)} %get-tuple-element.9, pred[80]{0:T(512)(128)(4,1)S(1)} %get-tuple-element.10), kind=kOutput, calls=%fused_computation.18 | convolution fusion | flops 178913280 | bytes 11862176 | tf_op jit(solution)/shard_map/tab,tbv->tav/dot_general | solution.py:59
  49.2 0.0 copy-start
  49.2 1.3 copy.15
  50.5 1.2 copy.16
  51.7 0.0 all-gather.6.cloned.1.call-update
  51.7 0.0 all-gather.8.cloned.1.call-start
  51.8 0.1 broadcast_in_dim.48
  51.9 0.0 copy-done
  52.0 0.0 collective-permute-done
  52.0 1.5 collective-permute-start.2
  53.6 0.0 collective-permute-done.1
  53.6 8.7 %collective-permute-done.2 = bf16[8192,16]{0,1:T(8,128)(2,1)S(1)} collective-permute-done((bf16[8192,16]{0,1:T(8,128)(2,1)S(1)}, bf16[8192,16]{0,1:T(8,128)(2,1)S(1)}, u32[]{:S(2)}, u32[]{:S(2)}) %collective-permute-start.2) | collective-permute-done | bytes 262176 | tf_op jit(solution)/shard_map/ppermute | solution.py:16
  62.4 0.1 copy.26
  62.5 0.6 gather_fusion.1
  63.1 0.0 copy-start.3
  63.1 0.0 copy-start.2
  63.1 0.0 copy-start.1
  63.1 5.6 %fusion.13 = bf16[80,256,16]{1,2,0:T(8,128)(2,1)S(1)} fusion(bf16[80,256,16]{1,2,0:T(8,128)(2,1)S(1)} %gather_fusion.1, bf16[1,1,80,256,256]{4,3,2,1,0:T(8,128)(2,1)} %param.4, pred[256,256]{1,0:T(8,128)(4,1)S(1)} %iota_compare_fusion, pred[80]{0:T(512)(128)(4,1)S(1)} %get-tuple-element.9, pred[80]{0:T(512)(128)(4,1)S(1)} %get-tuple-element.10), kind=kOutput, calls=%fused_computation.19 | convolution fusion | flops 178913280 | bytes 11862176 | tf_op jit(solution)/shard_map/tba,tbv->tav/dot_general | solution.py:62
  68.7 1.3 copy.18
  70.0 1.3 copy.19
  71.3 0.0 all-gather.8.cloned.1.call-update
  71.3 0.0 copy-done.3
  71.3 0.6 dynamic-slice.1
  72.0 0.0 copy-done.2
  72.0 0.7 dynamic-slice
  74.0 0.0 copy-done.1
  74.0 0.1 fusion.24
  74.1 7.2 %all-reduce.1 = s32[640]{0:T(1024)S(1)} all-reduce(s32[640]{0:T(1024)S(1)} %get-tuple-element.5), channel_id=1, replica_groups=mesh['row'=8,'col'=4] {'row'}, use_global_device_ids=true, to_apply=%add.1 | all-reduce | flops 640 | bytes 5120
  81.3 6.7 %all-reduce = s32[320]{0:T(512)S(1)} all-reduce(s32[320]{0:T(512)S(1)} %get-tuple-element.6), channel_id=1, replica_groups=mesh['row'=8,'col'=4] {'col'}, use_global_device_ids=true, to_apply=%add | all-reduce | flops 320 | bytes 2560
  88.0 18.8 %all-gather.6.cloned.1.call-done = bf16[320,4096]{1,0:T(8,128)(2,1)} async-done(((bf16[80,4096]{1,0:T(8,128)(2,1)}), bf16[320,4096]{1,0:T(8,128)(2,1)}) %all-gather.6.cloned.1.call-update) | async-done | bytes 2621456 | tf_op jit(solution)/shard_map/all_gather | solution.py:85
  106.9 2.4 %fusion.17 = f32[32,4096]{1,0:T(8,128)S(1)} fusion(bf16[320,4096]{1,0:T(8,128)(2,1)} %all-gather.6.cloned.1.call-done, s32[32]{0:T(128)S(1)} %iota_add_fusion, s32[320]{0:T(512)S(1)} %all-reduce), kind=kOutput, calls=%fused_computation.26 | convolution fusion | flops 83896320 | bytes 3147136 | tf_op jit(solution)/shard_map/ts,tk->sk/dot_general | solution.py:81
  109.3 39.3 %all-gather.8.cloned.1.call-done = bf16[640,4096]{1,0:T(8,128)(2,1)} async-done(((bf16[80,4096]{1,0:T(8,128)(2,1)}), bf16[640,4096]{1,0:T(8,128)(2,1)}) %all-gather.8.cloned.1.call-update) | async-done | bytes 5242896 | tf_op jit(solution)/shard_map/all_gather | solution.py:91
  148.6 3.5 %convolution_add_fusion = f32[32,4096]{1,0:T(8,128)S(1)} fusion(f32[32,4096]{1,0:T(8,128)S(1)} %fusion.17, bf16[640,4096]{1,0:T(8,128)(2,1)} %all-gather.8.cloned.1.call-done, s32[32]{0:T(128)S(1)} %iota_add_fusion, s32[640]{0:T(1024)S(1)} %all-reduce.1), kind=kOutput, calls=%fused_computation.14 | convolution fusion | flops 167923712 | bytes 6294144 | tf_op jit(solution)/shard_map/ts,tk->sk/dot_general | solution.py:81
  152.2 2.8 %add.131 = f32[8192,16]{1,0:T(8,128)} reshape(f32[32,4096]{1,0:T(8,128)S(1)} %convolution_add_fusion) | data formatting | bytes 1048576 | tf_op jit(solution)/shard_map/add | solution.py:97
  154.9 3.5 %copy.20 = f32[8192,16]{0,1:T(8,128)} copy(f32[8192,16]{1,0:T(8,128)} %add.131) | data formatting | bytes 1048576 | tf_op jit(solution)/shard_map/add | solution.py:97
  (11 shorter events, 0.2 us)
Async XLA Ops:
  6.5 33.4 %all-gather.4.cloned.1.call-start = ((), (), s32[]{:S(2)}) async-start(), calls=%async_computation | async-start | bytes 2359296 | tf_op jit(solution)/shard_map/all_gather | solution.py:52
  7.3 99.6 %all-gather.6.cloned.1.call-start = ((), (), s32[]{:S(2)}) async-start(), calls=%async_computation.1 | async-start | bytes 3276800 | tf_op jit(solution)/shard_map/all_gather | solution.py:85
  7.3 46.3 %collective-permute-start.1 = (bf16[8192,16]{0,1:T(8,128)(2,1)}, bf16[8192,16]{0,1:T(8,128)(2,1)S(1)}, u32[]{:S(2)}, u32[]{:S(2)}) collective-permute-start(bf16[8192,16]{0,1:T(8,128)(2,1)} %param.7), channel_id=1, source_target_pairs={{0,3},{1,0},{2,1},{3,2},{4,7},{5,4},{6,5},{7,6},{8,11},{9,8},{10,9... | collective-permute-start | bytes 786440 | tf_op jit(solution)/shard_map/ppermute | solution.py:21
  12.4 39.6 %collective-permute-start = (bf16[8192,16]{0,1:T(8,128)(2,1)}, bf16[8192,16]{0,1:T(8,128)(2,1)S(1)}, u32[]{:S(2)}, u32[]{:S(2)}) collective-permute-start(bf16[8192,16]{0,1:T(8,128)(2,1)} %param.7), channel_id=1, source_target_pairs={{0,1},{1,2},{2,3},{3,0},{4,5},{5,6},{6,7},{7,4},{8,9},{9,10},{10,1... | collective-permute-start | bytes 786440 | tf_op jit(solution)/shard_map/ppermute | solution.py:16
  49.2 2.7 %copy-start = (bf16[8192,16]{0,1:T(8,128)(2,1)S(1)}, bf16[8192,16]{0,1:T(8,128)(2,1)}, u32[]{:S(2)}) copy-start(bf16[8192,16]{0,1:T(8,128)(2,1)} %param.7) | copy-start | bytes 786436
  51.7 96.9 %all-gather.8.cloned.1.call-start = ((), (), s32[]{:S(2)}) async-start(), calls=%async_computation.2 | async-start | bytes 5898240 | tf_op jit(solution)/shard_map/all_gather | solution.py:91
  52.0 10.3 %collective-permute-start.2 = (bf16[8192,16]{0,1:T(8,128)(2,1)S(1)}, bf16[8192,16]{0,1:T(8,128)(2,1)S(1)}, u32[]{:S(2)}, u32[]{:S(2)}) collective-permute-start(bf16[8192,16]{0,1:T(8,128)(2,1)S(1)} %collective-permute-done), channel_id=1, source_target_pairs={{0,1},{1,2},{2,3},{3,0},{4,5},{5,6},{6,7},{7,4},{8,9},{9,10},{10,1... | collective-permute-start | bytes 786440 | tf_op jit(solution)/shard_map/ppermute | solution.py:16
  63.1 8.3 %copy-start.3 = (u32[32]{0:T(128)S(1)}, u32[32]{0:T(128)}, u32[]{:S(2)}) copy-start(u32[32]{0:T(128)} %constant.97) | copy-start | bytes 388
  63.1 8.9 %copy-start.2 = (u32[32]{0:T(128)S(1)}, u32[32]{0:T(128)}, u32[]{:S(2)}) copy-start(u32[32]{0:T(128)} %constant.92) | copy-start | bytes 388
  63.1 10.9 %copy-start.1 = (s32[2,1,1,80]{3,2,1,0:T(1,128)S(1)}, s32[2,1,1,80]{3,2,1,0:T(1,128)}, u32[]{:S(2)}) copy-start(s32[2,1,1,80]{3,2,1,0:T(1,128)} %param.5) | copy-start | bytes 1924
Sparse Core Ops, SparseCore 0:
  9.3 30.5 all-gather.3
  51.9 54.9 all-gather.5
  108.7 39.8 all-gather.7
